TPU v7x, 32 devices: a whole 2x2x4 slice. The times are simulated.
32 devices in a mesh: grp: 2 (over y), row: 4 (over z), col: 4 (over x, core).
Axes of the slice: x: 2, y: 2, z: 4, core: 2. Of those that a mesh axis runs over, the one named last changes fastest.
Arguments:
- pair: bfloat16 [512, 256, 128], P(('grp', 'row'), 'col'), parts along dimension 0, may hold values from -6 to 6
- cotangent: bfloat16 [512, 256, 128], P(('grp', 'row'), 'col'), parts along dimension 0, may hold values from -6 to 6
- tile_mask: int32 [4, 2], P('grp'), parts along dimension 0, may hold values 0 or 1
- chain_ids: int32 [512], P('grp'), parts along dimension 0, may hold values from 0 to 4, never falling along the last dimension, each value on 1 to 128 neighbouring positions
- gain_in: float32 [2, 128], replicated, may hold values from 0.1 to 1.9
- weight_in: bfloat16 [2, 128, 512], replicated, may hold values from -0.5 to 0.5
- weight_gate: bfloat16 [2, 128, 128], replicated, may hold values from -0.5 to 0.5
- gain_out: float32 [2, 128], replicated, may hold values from 0.1 to 1.9
- weight_out: bfloat16 [2, 128, 128], replicated, may hold values from -0.5 to 0.5
Outputs:
- grad_pair: bfloat16 [512, 256, 128], P(('grp', 'row'), 'col'), parts along dimension 0
- grad_weight_in: float32 [4, 128, 512], P('grp'), parts along dimension 0
- grad_weight_gate: float32 [4, 128, 128], P('grp'), parts along dimension 0
- grad_weight_out: float32 [4, 128, 128], P('grp'), parts along dimension 0
- grad_gain_in: float32 [4, 128], P('grp'), parts along dimension 0
- grad_gain_out: float32 [4, 128], P('grp'), parts along dimension 0
There are 2 independent parts, one for each index of `grp`. A program takes and returns all parts, laid end to end along the dimension named above; an argument that names none is the same for every part. Nothing has to cross between parts.
Inputs may be any that keep to these rules, and one draw needn't show every extreme that they name: `chain_ids`: chain ids never fall along the tokens.
All inputs are finite; a program needn't handle non-finite values.
Results may differ from a plain program's by a relative error of at most 0.023.
Values may be sent and summed in bfloat16 or wider, within the bound.
A program may use at most 192 MiB of HBM per device.

v0:
```python
import jax
import jax.numpy as jnp
from jax import lax
from jax.sharding import PartitionSpec as P

eps = 1e-05


def broadcast(value, axis, source):
    kept = jnp.where(lax.axis_index(axis) == source, value, 0).astype(value.dtype)
    return lax.psum(kept, axis)


def layer_normalize(values):
    average = jnp.mean(values, axis=-1, keepdims=True)
    centred = values - average
    inv_std = lax.rsqrt(jnp.mean(centred * centred, axis=-1, keepdims=True) + eps)
    return (centred * inv_std, inv_std)


def norm_backward_step(grad_hat, normed, inv_std):
    inner = jnp.mean(grad_hat * normed, axis=-1, keepdims=True)
    return inv_std * (grad_hat - jnp.mean(grad_hat, axis=-1, keepdims=True) - normed * inner)


def front(flat_rows, pair_mask, gain_vector, weight_proj, weight_gating):
    zhat, inv_std = layer_normalize(flat_rows.astype(jnp.float32))
    znorm = (zhat * gain_vector).astype(jnp.bfloat16)
    projected = jnp.dot(znorm, weight_proj, preferred_element_type=jnp.float32)
    width = weight_proj.shape[1] // 4
    left_lin = projected[:, :width]
    left_gate = jax.nn.sigmoid(projected[:, width : 2 * width])
    right_lin = projected[:, 2 * width : 3 * width]
    right_gate = jax.nn.sigmoid(projected[:, 3 * width :])
    left_edge = (pair_mask[:, None] * left_gate * left_lin).astype(jnp.bfloat16)
    right_edge = (right_gate * right_lin).astype(jnp.bfloat16)
    gating = jax.nn.sigmoid(jnp.dot(znorm, weight_gating, preferred_element_type=jnp.float32))
    return (
        zhat,
        inv_std,
        znorm,
        left_lin,
        left_gate,
        right_lin,
        right_gate,
        left_edge,
        right_edge,
        gating,
    )


def back_half(flat_rows, triangle_product, gating, gain_vector, weight_final):
    input_centred_scaled, input_inverse_deviation = layer_normalize(triangle_product)
    normalized_input = (input_centred_scaled * gain_vector).astype(jnp.bfloat16)
    triangle_update = jnp.dot(normalized_input, weight_final, preferred_element_type=jnp.float32)
    output_result = (flat_rows.astype(jnp.float32) + gating * triangle_update).astype(jnp.bfloat16)
    return (
        input_centred_scaled,
        input_inverse_deviation,
        normalized_input,
        triangle_update,
        output_result,
    )


def post_grad(incoming, gating, backward_values, gain_vector, weight_final):
    input_centred_scaled, input_inverse_deviation, normalized_input, triangle_update = (
        backward_values[0],
        backward_values[1],
        backward_values[2],
        backward_values[3],
    )
    grad_update = (incoming * gating).astype(jnp.bfloat16)
    grad_gating = (incoming * triangle_update * gating * (1.0 - gating)).astype(jnp.bfloat16)
    grad_wout = jnp.dot(normalized_input.T, grad_update, preferred_element_type=jnp.float32)
    gradient_normalized_input = jnp.dot(
        grad_update, weight_final.T, preferred_element_type=jnp.float32
    )
    gradient_gate_output = jnp.sum(gradient_normalized_input * input_centred_scaled, axis=0)
    gradient_triangle = norm_backward_step(
        gradient_normalized_input * gain_vector, input_centred_scaled, input_inverse_deviation
    ).astype(jnp.bfloat16)
    return (gradient_triangle, grad_gating, grad_wout, gradient_gate_output)


def pre_grad(
    incoming,
    grad_left,
    grad_right,
    grad_gating,
    front_vals,
    pair_mask,
    gain_vector,
    weight_proj,
    weight_gating,
):
    zhat, inv_std, znorm, left_lin, left_gate, right_lin, right_gate = front_vals[:7]
    masked = grad_left * pair_mask[:, None]
    grad_proj = jnp.concatenate(
        [
            masked * left_gate,
            masked * left_lin * left_gate * (1.0 - left_gate),
            grad_right * right_gate,
            grad_right * right_lin * right_gate * (1.0 - right_gate),
        ],
        axis=1,
    ).astype(jnp.bfloat16)
    grad_win = jnp.dot(znorm.T, grad_proj, preferred_element_type=jnp.float32)
    grad_wgate = jnp.dot(znorm.T, grad_gating, preferred_element_type=jnp.float32)
    grad_znorm = jnp.dot(grad_proj, weight_proj.T, preferred_element_type=jnp.float32)
    grad_znorm = grad_znorm + jnp.dot(
        grad_gating, weight_gating.T, preferred_element_type=jnp.float32
    )
    grad_gin = jnp.sum(grad_znorm * zhat, axis=0)
    grad_input = incoming + norm_backward_step(grad_znorm * gain_vector, zhat, inv_std)
    return (grad_input, grad_win, grad_wgate, grad_gin)


def local_mask(tile_mask, chain_ids, row_start, col_start, rows_dev, cols_dev):
    tile_count = tile_mask.shape[0]
    tile_size = chain_ids.shape[0] // tile_count
    row_ids = row_start + jnp.arange(rows_dev, dtype=jnp.int32)
    col_ids = col_start + jnp.arange(cols_dev, dtype=jnp.int32)
    tile_index = jnp.arange(tile_count, dtype=jnp.int32)
    row_hot = (row_ids[:, None] // tile_size == tile_index[None, :]).astype(jnp.float32)
    col_hot = (col_ids[:, None] // tile_size == tile_index[None, :]).astype(jnp.float32)
    tile_vals = jnp.dot(jnp.dot(row_hot, tile_mask.astype(jnp.float32)), col_hot.T)
    row_chain = lax.dynamic_slice_in_dim(chain_ids, row_start, rows_dev)
    col_chain = lax.dynamic_slice_in_dim(chain_ids, col_start, cols_dev)
    same_chain = (row_chain[:, None] == col_chain[None, :]).astype(jnp.float32)
    return jnp.maximum(tile_vals, same_chain).reshape(-1)


def column_panel(values):
    return lax.all_gather(values, "row", axis=0, tiled=True)


def row_panel(values):
    return lax.all_gather(values, "col", axis=1, tiled=True)


def row_sum(values):
    return lax.psum_scatter(
        values.astype(jnp.bfloat16), "col", scatter_dimension=1, tiled=True
    ).astype(jnp.float32)


def diagonal_block(col_panel, rows_dev):
    cols_dev = col_panel.shape[1]
    first_row = lax.axis_index("row") * rows_dev
    root_col = first_row // cols_dev
    offset = first_row % cols_dev
    received = broadcast(col_panel, "col", root_col)
    return lax.dynamic_slice_in_dim(received, offset, rows_dev, 1)


def per_device(
    pair, cotangent, tile_mask, chain_ids, gain_in, weight_in, weight_gate, gain_out, weight_out
):
    rows_dev, cols_dev, channels = pair.shape
    hidden = weight_out.shape[1]
    shape_hid = (rows_dev, cols_dev, hidden)
    row_start = lax.axis_index("row") * rows_dev
    col_start = lax.axis_index("col") * cols_dev
    pair_mask = local_mask(tile_mask, chain_ids, row_start, col_start, rows_dev, cols_dev)
    flat_one = pair.reshape(-1, channels)
    front_one = front(flat_one, pair_mask, gain_in[0], weight_in[0], weight_gate[0])
    left_one = front_one[7].reshape(shape_hid)
    right_one = front_one[8].reshape(shape_hid)
    right_cols = column_panel(right_one)
    partial_one = jnp.einsum(
        "ikh,jkh->ijh", left_one, right_cols, preferred_element_type=jnp.float32
    )
    tri_one = row_sum(partial_one).reshape(-1, hidden)
    back_one = back_half(flat_one, tri_one, front_one[9], gain_out[0], weight_out[0])
    flat_two = back_one[4]
    front_two = front(flat_two, pair_mask, gain_in[1], weight_in[1], weight_gate[1])
    left_two = front_two[7].reshape(shape_hid)
    right_two = front_two[8].reshape(shape_hid)
    edge_cols = column_panel(jnp.concatenate([left_two, right_two], axis=2))
    left_diag = diagonal_block(edge_cols[:, :, :hidden], rows_dev)
    tri_two = jnp.einsum(
        "kih,kjh->ijh", left_diag, edge_cols[:, :, hidden:], preferred_element_type=jnp.float32
    )
    back_two = back_half(
        flat_two, tri_two.reshape(-1, hidden), front_two[9], gain_out[1], weight_out[1]
    )
    cot_two = cotangent.reshape(-1, channels).astype(jnp.float32)
    post_two = post_grad(cot_two, front_two[9], back_two, gain_out[1], weight_out[1])
    dtri_two = post_two[0].reshape(shape_hid)
    grad_cols = column_panel(dtri_two)
    left_rows = row_panel(left_two)
    dright_two = jnp.einsum(
        "kih,ijh->kjh", left_rows, grad_cols, preferred_element_type=jnp.float32
    )
    dleft_two = row_sum(
        jnp.einsum("kjh,ijh->kih", right_two, grad_cols, preferred_element_type=jnp.float32)
    )
    pre_two = pre_grad(
        cot_two,
        dleft_two.reshape(-1, hidden),
        dright_two.reshape(-1, hidden),
        post_two[1],
        front_two,
        pair_mask,
        gain_in[1],
        weight_in[1],
        weight_gate[1],
    )
    cot_one = lax.optimization_barrier(pre_two[0].astype(jnp.bfloat16)).astype(jnp.float32)
    post_one = post_grad(cot_one, front_one[9], back_one, gain_out[0], weight_out[0])
    dtri_one = post_one[0].reshape(shape_hid)
    grad_rows = row_panel(dtri_one)
    dleft_one = jnp.einsum(
        "ijh,jkh->ikh", grad_rows, right_cols, preferred_element_type=jnp.float32
    )
    dright_one = lax.psum_scatter(
        jnp.einsum("ijh,ikh->jkh", grad_rows, left_one, preferred_element_type=jnp.float32).astype(
            jnp.bfloat16
        ),
        "row",
        scatter_dimension=0,
        tiled=True,
    ).astype(jnp.float32)
    pre_one = pre_grad(
        cot_one,
        dleft_one.reshape(-1, hidden),
        dright_one.reshape(-1, hidden),
        post_one[1],
        front_one,
        pair_mask,
        gain_in[0],
        weight_in[0],
        weight_gate[0],
    )
    totals = lax.psum(
        (
            jnp.stack([pre_one[1], pre_two[1]]),
            jnp.stack([pre_one[2], pre_two[2]]),
            jnp.stack([post_one[2], post_two[2]]),
            jnp.stack([pre_one[3], pre_two[3]]),
            jnp.stack([post_one[3], post_two[3]]),
        ),
        ("row", "col"),
    )
    factor = 1.0 / (rows_dev * lax.axis_size("row"))
    grad_pair = pre_one[0].astype(jnp.bfloat16).reshape(rows_dev, cols_dev, channels)
    return (
        grad_pair,
        totals[0] * factor,
        totals[1] * factor,
        totals[2] * factor,
        totals[3] * factor,
        totals[4] * factor,
    )


def solution(mesh):
    in_specs = (
        P(("grp", "row"), "col", None),
        P(("grp", "row"), "col", None),
        P("grp", None),
        P("grp"),
        P(),
        P(),
        P(),
        P(),
        P(),
    )
    out_specs = (
        P(("grp", "row"), "col", None),
        P("grp", None, None),
        P("grp", None, None),
        P("grp", None, None),
        P("grp", None),
        P("grp", None),
    )
    return jax.shard_map(
        per_device, mesh=mesh, in_specs=in_specs, out_specs=out_specs, check_vma=False
    )
```

profile of v0, /device:TPU:0, one launch (start us, length us, event | category | flops | bytes accessed | tf_op | source)
XLA Modules:
  0.0 1087.9 jit_solution(13493793226683913667)
XLA Ops:
  28.7 148.3 %all-gather.6.cloned.1.call-done = bf16[256,64,128]{1,0,2:T(8,128)(2,1)} async-done(((bf16[64,64,128]{1,0,2:T(8,128)(2,1)}), bf16[256,64,128]{1,0,2:T(8,128)(2,1)}) %all-gather.6.cloned.1.call-update) | async-done | bytes 4194320 | tf_op jit(solution)/shard_map/all_gather | solution.py:135
  177.0 8.4 convert_bitcast_fusion.2
  185.4 7.4 copy.216
  194.6 41.0 %reduce-scatter.4.cloned.1.call-done = bf16[64,64,128]{2,0,1:T(8,128)(2,1)} async-done(((bf16[64,256,128]{2,0,1:T(8,128)(2,1)}), bf16[64,64,128]{2,0,1:T(8,128)(2,1)}) %reduce-scatter.4.cloned.1.call-update) | async-done | bytes 1048592 | tf_op jit(solution)/shard_map/reduce_scatter | solution.py:143
  260.6 149.7 %all-gather.8.cloned.1.call-done = bf16[256,64,256]{2,1,0:T(8,128)(2,1)} async-done(((bf16[64,64,256]{2,1,0:T(8,128)(2,1)}), bf16[256,64,256]{2,1,0:T(8,128)(2,1)}) %all-gather.8.cloned.1.call-update) | async-done | bytes 8388624 | tf_op jit(solution)/shard_map/all_gather | solution.py:135
  410.3 6.5 fusion.90
  416.8 7.3 copy.272
  439.5 7.4 copy.271
  446.8 65.6 %all-reduce.5.cloned.1.call-done = bf16[256,64,128]{0,1,2:T(8,128)(2,1)} async-done(((bf16[256,64,128]{0,1,2:T(8,128)(2,1)}), bf16[256,64,128]{0,1,2:T(8,128)(2,1)}) %all-reduce.5.cloned.1.call-update) | async-done | bytes 4194320 | tf_op jit(solution)/shard_map/psum | solution.py:11
  512.5 6.8 fusion.92
  519.5 5.3 copy.232
  527.8 5.2 multiply_reduce_fusion.1
  549.6 142.2 %all-gather.10.cloned.1.call-done = bf16[256,64,128]{1,0,2:T(8,128)(2,1)} async-done(((bf16[64,64,128]{1,0,2:T(8,128)(2,1)}), bf16[256,64,128]{1,0,2:T(8,128)(2,1)}) %all-gather.10.cloned.1.call-update) | async-done | bytes 4194320 | tf_op jit(solution)/shard_map/all_gather | solution.py:135
  691.8 9.2 convert_bitcast_fusion.1
  701.0 7.4 copy.235
  708.8 17.2 %all-gather.12.cloned.1.call-done = bf16[64,256,128]{2,0,1:T(8,128)(2,1)} async-done(((bf16[64,64,128]{2,0,1:T(8,128)(2,1)}), bf16[64,256,128]{2,0,1:T(8,128)(2,1)}) %all-gather.12.cloned.1.call-update) | async-done | bytes 4194320 | tf_op jit(solution)/shard_map/all_gather | solution.py:139
  725.9 7.4 copy.240
  737.8 5.3 copy.245
  747.4 8.5 convolution_bitcast_fusion.2
  755.9 5.3 copy.241
  764.2 8.8 reduce-scatter.6.cloned.1.call-done
  779.3 5.9 multiply_convert_fusion.12
  801.0 34.6 %all-gather.14.cloned.1.call-done = bf16[64,256,128]{2,0,1:T(8,128)(2,1)} async-done(((bf16[64,64,128]{2,0,1:T(8,128)(2,1)}), bf16[64,256,128]{2,0,1:T(8,128)(2,1)}) %all-gather.14.cloned.1.call-update) | async-done | bytes 4194320 | tf_op jit(solution)/shard_map/all_gather | solution.py:139
  835.5 7.4 copy.251
  843.0 6.0 convert_bitcast_fusion
  849.0 7.4 copy.256
  869.0 8.3 convolution_bitcast_fusion.1
  877.3 5.6 copy.252
  885.9 47.5 %reduce-scatter.8.cloned.1.call-done = bf16[64,64,128]{2,1,0:T(8,128)(2,1)} async-done(((bf16[256,64,128]{2,1,0:T(8,128)(2,1)}), bf16[64,64,128]{2,1,0:T(8,128)(2,1)}) %reduce-scatter.8.cloned.1.call-update) | async-done | bytes 1048592 | tf_op jit(solution)/shard_map/reduce_scatter | solution.py:217
  938.9 5.7 multiply_convert_fusion.7
  952.2 32.7 %all-reduce = (f32[2,128]{1,0:T(2,128)S(1)}, f32[2,128]{1,0:T(2,128)S(1)}) all-reduce(f32[2,128]{1,0:T(2,128)S(1)} %pad_maximum_fusion.10, f32[2,128]{1,0:T(2,128)S(1)} %pad_maximum_fusion.11), channel_id=1, replica_groups=mesh['grp'=2,'row'=4,'col'=4] {'row','col'}, use_global_device_ids=true, to_apply=%region_25.26 | all-reduce | flops 512 | bytes 4096 | tf_op jit(solution)/shard_map/psum | solution.py:236
  986.9 88.7 %all-reduce.7.cloned.1.call-done = (f32[2,128,512]{2,1,0:T(8,128)}, f32[2,128,128]{2,1,0:T(8,128)}, f32[2,128,128]{2,1,0:T(8,128)}) async-done(((f32[2,128,512]{2,1,0:T(8,128)}, f32[2,128,128]{2,1,0:T(8,128)}, f32[2,128,128]{2,1,0:T(8,128)}), (f32[2,128,512]{2,1,0:T(8,128)}, f32[2,128,128]{2,1,0:T(8,128)}, f32[2,128,128]{2,1,0:T(8,128)})) %all-reduce.7.cloned.1.call-update) | async-done | bytes 786448 | tf_op jit(solution)/shard_map/psum | solution.py:236
  (202 shorter events, 152.5 us)
Async XLA Ops:
  7.2 4.8 copy-start.16
  7.2 169.8 %all-gather.6.cloned.1.call-start = ((), (), s32[]{:S(2)}) async-start(), calls=%async_computation.3 | async-start | bytes 10485760 | tf_op jit(solution)/shard_map/all_gather | solution.py:135
  10.0 5.5 copy-start.34
  16.8 3.2 copy-start
  24.5 211.2 %reduce-scatter.4.cloned.1.call-start = ((), (), s32[]{:S(2)}) async-start(), calls=%async_computation.4 | async-start | bytes 5242880 | tf_op jit(solution)/shard_map/reduce_scatter | solution.py:143
  28.7 156.7 %copy-start.11 = (bf16[64,64,128]{0,1,2:T(8,128)(2,1)}, bf16[64,64,128]{0,1,2:T(8,128)(2,1)S(1)}, u32[]{:S(2)}) copy-start(bf16[64,64,128]{0,1,2:T(8,128)(2,1)S(1)} %copy.254) | copy-start | bytes 3145732
  192.9 217.5 %all-gather.8.cloned.1.call-start = ((), (), s32[]{:S(2)}) async-start(), calls=%async_computation.5 | async-start | bytes 10485760 | tf_op jit(solution)/shard_map/all_gather | solution.py:135
  194.6 48.5 %copy-start.35 = (bf16[2,128,128]{2,1,0:T(8,128)(2,1)S(1)}, bf16[2,128,128]{2,1,0:T(8,128)(2,1)}, u32[]{:S(2)}) copy-start(bf16[2,128,128]{2,1,0:T(8,128)(2,1)} %param.17) | copy-start | bytes 196612
  235.7 4.7 copy-start.6
  244.3 2.3 copy-start.20
  248.9 3.8 copy-start.1
  260.5 251.9 %all-reduce.5.cloned.1.call-start = ((), (), s32[]{:S(2)}) async-start(), calls=%async_computation.6 | async-start | bytes 8388608 | tf_op jit(solution)/shard_map/psum | solution.py:11
  428.6 263.2 %all-gather.10.cloned.1.call-start = ((), (), s32[]{:S(2)}) async-start(), calls=%async_computation.7 | async-start | bytes 10485760 | tf_op jit(solution)/shard_map/all_gather | solution.py:135
  527.8 5.3 copy-start.15
  541.9 184.1 %all-gather.12.cloned.1.call-start = ((), (), s32[]{:S(2)}) async-start(), calls=%async_computation.9 | async-start | bytes 5242880 | tf_op jit(solution)/shard_map/all_gather | solution.py:139
  544.9 228.1 %reduce-scatter.6.cloned.1.call-start = ((), (), s32[]{:S(2)}) async-start(), calls=%async_computation.8 | async-start | bytes 5242880 | tf_op jit(solution)/shard_map/reduce_scatter | solution.py:143
  708.4 127.1 %all-gather.14.cloned.1.call-start = ((), (), s32[]{:S(2)}) async-start(), calls=%async_computation.10 | async-start | bytes 5242880 | tf_op jit(solution)/shard_map/all_gather | solution.py:139
  743.2 4.3 copy-start.17
  785.3 2.4 copy-start.28
  790.0 2.3 copy-start.13
  790.0 2.3 copy-start.36
  790.7 5.1 copy-start.3
  800.9 132.4 %reduce-scatter.8.cloned.1.call-start = ((), (), s32[]{:S(2)}) async-start(), calls=%async_computation.11 | async-start | bytes 5242880 | tf_op jit(solution)/shard_map/reduce_scatter | solution.py:217
  856.4 219.2 %all-reduce.7.cloned.1.call-start = ((), (), s32[]{:S(2)}) async-start(), calls=%async_computation.12 | async-start | bytes 1572864 | tf_op jit(solution)/shard_map/psum | solution.py:236
  856.9 4.4 copy-start.25
  859.0 2.3 copy-start.4
  859.0 2.5 copy-start.14
  861.5 2.2 copy-start.21
  864.2 2.2 copy-start.27
  864.2 2.5 copy-start.29
  866.7 2.3 copy-start.2
  949.9 35.0 %copy-start.37 = (f32[1,128,512]{2,1,0:T(8,128)S(1)}, f32[1,128,512]{2,1,0:T(8,128)}, u32[]{:S(2)}) copy-start(f32[1,128,512]{2,1,0:T(8,128)} %convolution_bitcast_fusion.3) | copy-start | bytes 786436
  (20 other events, 28.8 us)
Sparse Core Ops, SparseCore 0:
  24.6 152.3 all-gather.5
  193.0 42.6 reduce-scatter.3
  260.7 149.6 all-gather.7
  428.7 83.7 all-reduce.4
  542.0 149.7 all-gather.9
  693.2 32.6 all-gather.11
  728.5 44.4 reduce-scatter.5
  801.0 34.4 all-gather.13
  856.6 76.7 reduce-scatter.7
  985.9 89.6 all-reduce.6
where the time goes:
time: 1100 us; the launch traced here: 1090 us
  waiting for transfers between devices  744 us (68%)
  local copies, waits for them, and re-layouts  143 us (13%)
  matrix products  84 us (8%)
  other arithmetic  68.2 us (6%)
  blocking collectives  32.7 us (3%)
  between operations  15.3 us (1%)
    all_gather x3, waiting for transfers between devices, column_panel(): return lax.all_gather(values, 'row', axis=0, tiled=True)  440 us
    psum x1, waiting for transfers between devices, per_device(): lax.psum((jnp.stack([pre_one[1], pre_two[1]]), jnp.stack([pre_one[2], pre...  88.7 us
    psum x1, waiting for transfers between devices, broadcast(): return lax.psum(kept, axis)  65.6 us
    all_gather x2, waiting for transfers between devices, row_panel(): return lax.all_gather(values, 'col', axis=1, tiled=True)  51.7 us
    reduce_scatter x2, waiting for transfers between devices, row_sum(): lax.psum_scatter(values.astype(jnp.bfloat16), 'col', scatter_dimension=1,...  49.8 us
    reduce_scatter x1, waiting for transfers between devices, per_device(): lax.psum_scatter(jnp.einsum('ijh,ikh->jkh', grad_rows, left_one, preferre...  47.5 us
    psum x1, blocking collectives, per_device(): lax.psum((jnp.stack([pre_one[1], pre_two[1]]), jnp.stack([pre_one[2], pre...  32.7 us
    unnamed x86, local copies, waits for them, and re-layouts  27.3 us
  transfers between devices with their start and end apart: 10, of which 10 were waited for; matrix products, arithmetic and copies ran while one was open for 10% of the time, Pallas kernels for 0%

commit v1 on v0

v1 whole, which is shorter than its diff:
```python
import jax
import jax.numpy as jnp
from jax import lax
from jax.sharding import PartitionSpec as P

eps = 1e-05
axes = ("row", "col")


def contract(a, b, dim_a, dim_b):
    return lax.dot_general(a, b, (((dim_a,), (dim_b,)), ((), ())), preferred_element_type=jnp.float32)


def layer_normalize(values):
    average = jnp.mean(values, axis=0, keepdims=True)
    centred = values - average
    inv_std = lax.rsqrt(jnp.mean(centred * centred, axis=0, keepdims=True) + eps)
    return (centred * inv_std, inv_std)


def norm_backward_step(grad_hat, normed, inv_std):
    inner = jnp.mean(grad_hat * normed, axis=0, keepdims=True)
    return inv_std * (grad_hat - jnp.mean(grad_hat, axis=0, keepdims=True) - normed * inner)


def front(cells, pair_mask, gain, weight_proj, weight_gating):
    zhat, inv_std = layer_normalize(cells)
    znorm = (zhat * gain[:, None]).astype(jnp.bfloat16)
    projected = contract(weight_proj, znorm, 0, 0)
    width = weight_proj.shape[1] // 4
    left_lin = projected[:width]
    left_gate = jax.nn.sigmoid(projected[width : 2 * width])
    right_lin = projected[2 * width : 3 * width]
    right_gate = jax.nn.sigmoid(projected[3 * width :])
    left = (pair_mask * left_gate * left_lin).astype(jnp.bfloat16)
    right = (right_gate * right_lin).astype(jnp.bfloat16)
    gating = jax.nn.sigmoid(contract(weight_gating, znorm, 0, 0))
    return (zhat, inv_std, znorm, left_lin, left_gate, right_lin, right_gate, left, right, gating)


def back_half(cells, tri, gating, gain, weight_final):
    xhat, inv_std = layer_normalize(tri)
    xnorm = (xhat * gain[:, None]).astype(jnp.bfloat16)
    update = contract(weight_final, xnorm, 0, 0)
    result = (cells + gating * update).astype(jnp.bfloat16)
    return (xhat, inv_std, xnorm, update, result)


def post_grad(incoming, gating, backs, gain, weight_final):
    xhat, inv_std, xnorm, update = backs[:4]
    grad_update = (incoming * gating).astype(jnp.bfloat16)
    grad_gating = (incoming * update * gating * (1.0 - gating)).astype(jnp.bfloat16)
    grad_wout = contract(xnorm, grad_update, 1, 1)
    grad_xnorm = contract(weight_final, grad_update, 1, 0)
    grad_gout = jnp.sum(grad_xnorm * xhat, axis=1)
    grad_tri = norm_backward_step(grad_xnorm * gain[:, None], xhat, inv_std).astype(jnp.bfloat16)
    return (grad_tri, grad_gating, grad_wout, grad_gout)


def pre_grad(
    incoming, grad_left, grad_right, grad_gating, fronts, pair_mask, gain, weight_proj, weight_gating
):
    zhat, inv_std, znorm, left_lin, left_gate, right_lin, right_gate = fronts[:7]
    masked = grad_left * pair_mask
    grad_proj = jnp.concatenate(
        [
            masked * left_gate,
            masked * left_lin * left_gate * (1.0 - left_gate),
            grad_right * right_gate,
            grad_right * right_lin * right_gate * (1.0 - right_gate),
        ],
        axis=0,
    ).astype(jnp.bfloat16)
    grad_win = contract(znorm, grad_proj, 1, 1)
    grad_wgate = contract(znorm, grad_gating, 1, 1)
    grad_znorm = contract(weight_proj, grad_proj, 1, 0)
    grad_znorm = grad_znorm + contract(weight_gating, grad_gating, 1, 0)
    grad_gin = jnp.sum(grad_znorm * zhat, axis=1)
    grad_input = incoming + norm_backward_step(grad_znorm * gain[:, None], zhat, inv_std)
    return (grad_input, grad_win, grad_wgate, grad_gin)


def local_mask(tile_mask, chain_ids, row_start, col_start, rows_dev, cols_dev):
    tile_count = tile_mask.shape[0]
    tile_size = chain_ids.shape[0] // tile_count
    row_ids = row_start + jnp.arange(rows_dev, dtype=jnp.int32)
    col_ids = col_start + jnp.arange(cols_dev, dtype=jnp.int32)
    tile_index = jnp.arange(tile_count, dtype=jnp.int32)
    row_hot = (row_ids[:, None] // tile_size == tile_index[None, :]).astype(jnp.float32)
    col_hot = (col_ids[:, None] // tile_size == tile_index[None, :]).astype(jnp.float32)
    tile_vals = jnp.dot(jnp.dot(row_hot, tile_mask.astype(jnp.float32)), col_hot.T)
    row_chain = lax.dynamic_slice_in_dim(chain_ids, row_start, rows_dev)
    col_chain = lax.dynamic_slice_in_dim(chain_ids, col_start, cols_dev)
    same_chain = (row_chain[:, None] == col_chain[None, :]).astype(jnp.float32)
    return jnp.maximum(tile_vals, same_chain).reshape(1, -1)


def per_device(
    pair, cotangent, tile_mask, chain_ids, gain_in, weight_in, weight_gate, gain_out, weight_out
):
    rows_dev, cols_dev, channels = pair.shape
    hidden = weight_out.shape[1]
    grid_rows, grid_cols = lax.axis_size("row"), lax.axis_size("col")
    peers = grid_rows * grid_cols
    share = hidden // peers
    tokens = rows_dev * grid_rows
    cells_dev = rows_dev * cols_dev

    def exchange(blocks):
        return lax.all_to_all(blocks, axes, 0, 0)

    def to_channels(*arrays):
        sent = jnp.concatenate([a.reshape(peers, share, cells_dev) for a in arrays], axis=1)
        got = exchange(sent).reshape(grid_rows, grid_cols, len(arrays) * share, rows_dev, cols_dev)
        whole = got.transpose(2, 0, 3, 1, 4).reshape(len(arrays) * share, tokens, tokens)
        return [whole[n * share : (n + 1) * share] for n in range(len(arrays))]

    def to_cells(*arrays):
        stacked = jnp.concatenate([a.astype(jnp.bfloat16) for a in arrays], axis=0)
        split = stacked.reshape(-1, grid_rows, rows_dev, grid_cols, cols_dev)
        sent = split.transpose(1, 3, 0, 2, 4).reshape(peers, -1, cells_dev)
        got = exchange(sent).reshape(peers, len(arrays), share, cells_dev)
        return [got[:, n].reshape(hidden, cells_dev).astype(jnp.float32) for n in range(len(arrays))]

    def triangle(spec, a, b):
        return jnp.einsum(spec, a, b, preferred_element_type=jnp.float32)

    row_start = lax.axis_index("row") * rows_dev
    col_start = lax.axis_index("col") * cols_dev
    pair_mask = local_mask(tile_mask, chain_ids, row_start, col_start, rows_dev, cols_dev)
    cells_one = pair.reshape(-1, channels).T.astype(jnp.float32)
    front_one = front(cells_one, pair_mask, gain_in[0], weight_in[0], weight_gate[0])
    left_one, right_one = to_channels(front_one[7], front_one[8])
    (tri_one,) = to_cells(triangle("hik,hjk->hij", left_one, right_one))
    back_one = back_half(cells_one, tri_one, front_one[9], gain_out[0], weight_out[0])
    cells_two = back_one[4].astype(jnp.float32)
    front_two = front(cells_two, pair_mask, gain_in[1], weight_in[1], weight_gate[1])
    left_two, right_two = to_channels(front_two[7], front_two[8])
    (tri_two,) = to_cells(triangle("hki,hkj->hij", left_two, right_two))
    back_two = back_half(cells_two, tri_two, front_two[9], gain_out[1], weight_out[1])
    cot_two = cotangent.reshape(-1, channels).T.astype(jnp.float32)
    post_two = post_grad(cot_two, front_two[9], back_two, gain_out[1], weight_out[1])
    (dtri_two,) = to_channels(post_two[0])
    dleft_two, dright_two = to_cells(
        triangle("hkj,hij->hki", right_two, dtri_two), triangle("hki,hij->hkj", left_two, dtri_two)
    )
    pre_two = pre_grad(
        cot_two,
        dleft_two,
        dright_two,
        post_two[1],
        front_two,
        pair_mask,
        gain_in[1],
        weight_in[1],
        weight_gate[1],
    )
    cot_one = pre_two[0].astype(jnp.bfloat16).astype(jnp.float32)
    post_one = post_grad(cot_one, front_one[9], back_one, gain_out[0], weight_out[0])
    (dtri_one,) = to_channels(post_one[0])
    dleft_one, dright_one = to_cells(
        triangle("hij,hjk->hik", dtri_one, right_one), triangle("hij,hik->hjk", dtri_one, left_one)
    )
    pre_one = pre_grad(
        cot_one,
        dleft_one,
        dright_one,
        post_one[1],
        front_one,
        pair_mask,
        gain_in[0],
        weight_in[0],
        weight_gate[0],
    )
    grad_pair = pre_one[0].astype(jnp.bfloat16).T.reshape(rows_dev, cols_dev, channels)

    factor = 1.0 / tokens
    pieces = []
    for pre, post in ((pre_one, post_one), (pre_two, post_two)):
        pieces += [pre[1][:, n * hidden : (n + 1) * hidden] for n in range(4)] + [pre[2], post[2].T]
    pieces += [pre_one[3][None], pre_two[3][None], post_one[3][None], post_two[3][None]]
    stacked = jnp.concatenate(pieces, axis=0) * factor
    rows = stacked.shape[0]
    padded = jnp.pad(stacked, ((0, -rows % peers), (0, 0))).astype(jnp.bfloat16)
    parts = exchange(padded.reshape(peers, -1, channels))
    summed = jnp.sum(parts.astype(jnp.float32), axis=0).astype(jnp.bfloat16)
    totals = exchange(jnp.broadcast_to(summed, (peers,) + summed.shape))
    totals = totals.reshape(-1, channels)[:rows].astype(jnp.float32)
    blocks = totals[: 12 * channels].reshape(2, 6, channels, channels)
    gains = totals[12 * channels :]
    return (
        grad_pair,
        jnp.concatenate([blocks[:, n] for n in range(4)], axis=2),
        blocks[:, 4],
        blocks[:, 5].transpose(0, 2, 1),
        gains[:2],
        gains[2:4],
    )


def solution(mesh):
    in_specs = (
        P(("grp", "row"), "col", None),
        P(("grp", "row"), "col", None),
        P("grp", None),
        P("grp"),
        P(),
        P(),
        P(),
        P(),
        P(),
    )
    out_specs = (
        P(("grp", "row"), "col", None),
        P("grp", None, None),
        P("grp", None, None),
        P("grp", None, None),
        P("grp", None),
        P("grp", None),
    )
    return jax.shard_map(
        per_device, mesh=mesh, in_specs=in_specs, out_specs=out_specs, check_vma=False
    )
```

time: 1100 us -> 632 us (0.57)
  waiting for transfers between devices: 744 us -> 119 us
  blocking collectives: 32.7 us -> 178 us
  local copies, waits for them, and re-layouts: 143 us -> 180 us
  starting transfers between devices: 1.46 us -> 36.3 us
  matrix products: 84 us -> 51.9 us
  between operations: 15.3 us -> 1.98 us
    all_gather x5 -> x0, waiting for transfers between devices: 492 us -> none  [the longest x3 440 us: column_panel(): return lax.all_gather(values, 'row', axis=0, tiled=True)]
    all_to_all x0 -> x4, blocking collectives: none -> 178 us  [exchange(): return lax.all_to_all(blocks, axes, 0, 0)]
    psum x2 -> x0, waiting for transfers between devices: 154 us -> none  [the longest x1 88.7 us: per_device(): lax.psum((jnp.stack([pre_one[1], pre_two[1]]), jnp.stack([pre_one[2], pre...]
    all_to_all x0 -> x6, waiting for transfers between devices: none -> 119 us  [exchange(): return lax.all_to_all(blocks, axes, 0, 0)]
    reduce_scatter x3 -> x0, waiting for transfers between devices: 97.3 us -> none  [the longest x2 49.8 us: row_sum(): lax.psum_scatter(values.astype(jnp.bfloat16), 'col', scatter_dimension=1,...]
    reshape x10 -> x24, local copies, waits for them, and re-layouts: 33 us -> 126 us  [the longest x8 53 us: to_channels(): exchange(sent)]
    all_to_all x0 -> x6, starting transfers between devices: none -> 36.3 us  [exchange(): return lax.all_to_all(blocks, axes, 0, 0)]
    psum x1 -> x0, blocking collectives: 32.7 us -> none  [per_device(): lax.psum((jnp.stack([pre_one[1], pre_two[1]]), jnp.stack([pre_one[2], pre...]
  transfers between devices with their start and end apart: 10 -> 6, of which waited for: 10 -> 6; matrix products, arithmetic and copies ran while one was open for 10% -> 6% of each run, Pallas kernels for 0% -> 0%
where the time goes in v1:
time: 632 us; the launch traced here: 625 us
  local copies, waits for them, and re-layouts  180 us (28%)
  blocking collectives  178 us (28%)
  waiting for transfers between devices  119 us (19%)
  other arithmetic  58.6 us (9%)
  matrix products  51.9 us (8%)
  starting transfers between devices  36.3 us (6%)
    all_to_all x4, blocking collectives, exchange(): return lax.all_to_all(blocks, axes, 0, 0)  178 us
    all_to_all x6, waiting for transfers between devices, exchange(): return lax.all_to_all(blocks, axes, 0, 0)  119 us
    reshape x8, local copies, waits for them, and re-layouts, to_channels(): exchange(sent)  53 us
    reshape x8, local copies, waits for them, and re-layouts, to_cells(): split = stacked.reshape(-1, grid_rows, rows_dev, grid_cols, cols_dev)  40.6 us
    dot_general x18, matrix products, contract(): lax.dot_general(a, b, (((dim_a,), (dim_b,)), ((), ())), preferred_element...  40 us
    all_to_all x6, starting transfers between devices, exchange(): return lax.all_to_all(blocks, axes, 0, 0)  36.3 us
    slice x6, local copies, waits for them, and re-layouts, to_channels(): return [whole[n * share:(n + 1) * share] for n in range(len(arrays))]  23.4 us
    reshape x4, local copies, waits for them, and re-layouts, to_cells(): sent = split.transpose(1, 3, 0, 2, 4).reshape(peers, -1, cells_dev)  21.6 us
  transfers between devices with their start and end apart: 6, of which 6 were waited for; matrix products, arithmetic and copies ran while one was open for 6% of the time, Pallas kernels for 0%

profile of v1, /device:TPU:0, one launch (start us, length us, event | category | flops | bytes accessed | tf_op | source)
XLA Modules:
  0.0 625.1 jit_solution(2212542367484944051)
XLA Ops:
  17.8 55.0 %all_to_all.50 = bf16[16,16,4096]{2,1,0:T(8,128)(2,1)} all-to-all(bf16[16,16,4096]{2,1,0:T(8,128)(2,1)S(1)} %pad_maximum_fusion.2), channel_id=1, replica_groups=mesh['grp'=2,'row'=4,'col'=4] {'row','col'}, dimensions={0} | all-to-all | bytes 4194304 | tf_op jit(solution)/shard_map/all_to_all | solution.py:110
  72.8 6.9 %reshape.326 = bf16[4,4,16,64,64]{4,3,2,1,0:T(8,128)(2,1)} reshape(bf16[16,16,4096]{2,1,0:T(8,128)(2,1)} %all_to_all.50) | data formatting | bytes 4194304 | tf_op jit(solution)/shard_map/reshape | solution.py:114
  79.7 10.5 %copy.81 = bf16[4,4,16,64,64]{4,1,3,0,2:T(4,128)(2,1)S(1)} copy(bf16[4,4,16,64,64]{4,3,2,1,0:T(8,128)(2,1)} %reshape.326) | data formatting | bytes 4194304 | tf_op jit(solution)/shard_map/reshape | solution.py:114
  96.8 4.7 slice.167
  116.3 5.1 all-to-all-start.1
  124.7 19.7 %all-to-all-done.1 = bf16[16,8,4096]{2,1,0:T(8,128)(2,1)S(1)} async-done(((bf16[16,8,4096]{2,1,0:T(8,128)(2,1)}), bf16[16,8,4096]{2,1,0:T(8,128)(2,1)S(1)}, u32[]{:S(2)}, u32[]{:S(2)}) %all-to-all-start.1) | async-done | bytes 1048608 | tf_op jit(solution)/shard_map/all_to_all | solution.py:110
  160.9 54.3 %all_to_all.51 = bf16[16,16,4096]{2,1,0:T(8,128)(2,1)} all-to-all(bf16[16,16,4096]{2,1,0:T(8,128)(2,1)S(1)} %pad_maximum_fusion.3), channel_id=1, replica_groups=mesh['grp'=2,'row'=4,'col'=4] {'row','col'}, dimensions={0} | all-to-all | bytes 4194304 | tf_op jit(solution)/shard_map/all_to_all | solution.py:110
  215.2 6.9 %reshape.331 = bf16[4,4,16,64,64]{4,3,2,1,0:T(8,128)(2,1)} reshape(bf16[16,16,4096]{2,1,0:T(8,128)(2,1)} %all_to_all.51) | data formatting | bytes 4194304 | tf_op jit(solution)/shard_map/reshape | solution.py:114
  222.1 10.5 %copy.80 = bf16[4,4,16,64,64]{4,1,3,0,2:T(4,128)(2,1)S(1)} copy(bf16[4,4,16,64,64]{4,3,2,1,0:T(8,128)(2,1)} %reshape.331) | data formatting | bytes 4194304 | tf_op jit(solution)/shard_map/reshape | solution.py:114
  240.1 4.7 slice.177
  259.9 5.1 all-to-all-start.3
  265.1 5.0 fusion.39
  270.1 18.0 %all-to-all-done.3 = bf16[16,8,4096]{2,1,0:T(8,128)(2,1)} async-done(((bf16[16,8,4096]{2,1,0:T(8,128)(2,1)}), bf16[16,8,4096]{2,1,0:T(8,128)(2,1)}, u32[]{:S(2)}, u32[]{:S(2)}) %all-to-all-start.3) | async-done | bytes 1048608 | tf_op jit(solution)/shard_map/all_to_all | solution.py:110
  295.7 31.8 %all_to_all.52 = bf16[16,8,4096]{2,1,0:T(8,128)(2,1)} all-to-all(bf16[16,8,4096]{2,1,0:T(8,128)(2,1)S(1)} %fusion.105), channel_id=1, replica_groups=mesh['grp'=2,'row'=4,'col'=4] {'row','col'}, dimensions={0} | all-to-all | bytes 2097152 | tf_op jit(solution)/shard_map/all_to_all | solution.py:110
  331.7 4.8 copy.83
  345.0 7.1 %reshape.337 = bf16[16,4,64,4,64]{4,3,2,1,0:T(4,128)(2,1)} reshape(bf16[16,256,256]{2,1,0:T(8,128)(2,1)} %pad_maximum_fusion.4) | data formatting | bytes 4194304 | tf_op jit(solution)/shard_map/reshape | solution.py:120
  352.1 5.3 copy.79
  357.4 6.6 %reshape.338 = bf16[16,16,4096]{2,1,0:T(8,128)(2,1)} reshape(bf16[4,4,16,64,64]{4,3,2,1,0:T(8,128)(2,1)} %bitcast.355) | data formatting | bytes 4194304 | tf_op jit(solution)/shard_map/reshape | solution.py:121
  364.0 5.3 all-to-all-start.5
  374.6 35.8 %all-to-all-done.5 = bf16[16,16,4096]{2,1,0:T(8,128)(2,1)} async-done(((bf16[16,16,4096]{2,1,0:T(8,128)(2,1)}), bf16[16,16,4096]{2,1,0:T(8,128)(2,1)}, u32[]{:S(2)}, u32[]{:S(2)}) %all-to-all-start.5) | async-done | bytes 2097184 | tf_op jit(solution)/shard_map/all_to_all | solution.py:110
  420.2 5.6 multiply_convert_fusion.7
  436.9 36.4 %all_to_all.53 = bf16[16,8,4096]{2,1,0:T(8,128)(2,1)} all-to-all(bf16[16,8,4096]{2,1,0:T(8,128)(2,1)S(1)} %fusion.108), channel_id=1, replica_groups=mesh['grp'=2,'row'=4,'col'=4] {'row','col'}, dimensions={0} | all-to-all | bytes 2097152 | tf_op jit(solution)/shard_map/all_to_all | solution.py:110
  477.5 4.9 copy.82
  490.8 7.1 %reshape.343 = bf16[16,4,64,4,64]{4,3,2,1,0:T(4,128)(2,1)} reshape(bf16[16,256,256]{2,1,0:T(8,128)(2,1)} %pad_maximum_fusion.5) | data formatting | bytes 4194304 | tf_op jit(solution)/shard_map/reshape | solution.py:120
  497.9 5.3 copy.78
  503.2 6.6 %reshape.344 = bf16[16,16,4096]{2,1,0:T(8,128)(2,1)} reshape(bf16[4,4,16,64,64]{4,3,2,1,0:T(8,128)(2,1)} %bitcast.356) | data formatting | bytes 4194304 | tf_op jit(solution)/shard_map/reshape | solution.py:121
  509.9 5.2 all-to-all-start.7
  526.3 29.9 %all-to-all-done.7 = bf16[16,16,4096]{2,1,0:T(8,128)(2,1)} async-done(((bf16[16,16,4096]{2,1,0:T(8,128)(2,1)}), bf16[16,16,4096]{2,1,0:T(8,128)(2,1)}, u32[]{:S(2)}, u32[]{:S(2)}) %all-to-all-start.7) | async-done | bytes 2097184 | tf_op jit(solution)/shard_map/all_to_all | solution.py:110
  565.0 5.1 multiply_convert_fusion.3
  577.7 11.4 %all-to-all-start.8 = ((bf16[16,97,128]{2,1,0:T(8,128)(2,1)}), bf16[16,97,128]{2,1,0:T(8,128)(2,1)}, u32[]{:S(2)}, u32[]{:S(2)}) async-start(bf16[16,97,128]{2,1,0:T(8,128)(2,1)} %reshape.347), calls=%async_computation.8 | async-start | bytes 851968 | tf_op jit(solution)/shard_map/all_to_all | solution.py:110
  590.5 11.3 %all-to-all-done.8 = bf16[16,97,128]{2,1,0:T(8,128)(2,1)} async-done(((bf16[16,97,128]{2,1,0:T(8,128)(2,1)}), bf16[16,97,128]{2,1,0:T(8,128)(2,1)}, u32[]{:S(2)}, u32[]{:S(2)}) %all-to-all-start.8) | async-done | bytes 397344 | tf_op jit(solution)/shard_map/all_to_all | solution.py:110
  608.1 8.9 %fusion.93 = bf16[4096,128]{1,0:T(8,128)(2,1)} fusion(bf16[64,64,128]{2,1,0:T(8,128)(2,1)S(1)} %copy-done.2, f32[4096,128]{1,0:T(8,128)} %get-tuple-element.76, f32[4096,128]{1,0:T(8,128)S(1)} %copy-done.5, f32[4096,128]{1,0:T(8,128)} %get-tuple-element.70, f32[4096,128]{1,0:T(8,128)} %copy-done.7, f32[4096]{0:T(1024)S(1)} %broadcast_multiply_fusion.1, ...), kind=kLoop, calls=%fused_computation.137 | loop fusion | flops 13107200 | bytes 11666432 | tf_op jit(solution)/shard_map/convert_element_type | solution.py:175
  (254 shorter events, 182.2 us)
Async XLA Ops:
  0.6 5.2 copy-start.69
  2.6 5.1 copy-start.36
  4.6 567.7 %copy-start.34 = (f32[4096]{0:T(1024)}, f32[4096]{0:T(1024)S(1)}, u32[]{:S(2)}) copy-start(f32[4096]{0:T(1024)S(1)} %div.96) | copy-start | bytes 49156
  5.9 566.4 %copy-start.37 = (f32[4096]{0:T(1024)}, f32[4096]{0:T(1024)S(1)}, u32[]{:S(2)}) copy-start(f32[4096]{0:T(1024)S(1)} %add_rsqrt_fusion.3) | copy-start | bytes 49156
  7.7 114.9 %copy-start.8 = (bf16[128,4096]{0,1:T(8,128)(2,1)}, bf16[128,4096]{0,1:T(8,128)(2,1)S(1)}, u32[]{:S(2)}) copy-start(bf16[128,4096]{0,1:T(8,128)(2,1)S(1)} %fusion.85) | copy-start | bytes 3145732
  96.8 7.4 %copy-start.11 = (bf16[8,256,256]{2,1,0:T(8,128)(2,1)}, bf16[8,256,256]{2,1,0:T(8,128)(2,1)S(1)}, u32[]{:S(2)}) copy-start(bf16[8,256,256]{2,1,0:T(8,128)(2,1)S(1)} %slice.165) | copy-start | bytes 3145732
  112.1 9.3 %copy-start.68 = (f32[2,128]{1,0:T(2,128)S(1)}, f32[2,128]{1,0:T(2,128)}, u32[]{:S(2)}) copy-start(f32[2,128]{1,0:T(2,128)} %param.16) | copy-start | bytes 3076
  112.1 10.4 %copy-start.48 = (bf16[2,128,128]{2,1,0:T(8,128)(2,1)S(1)}, bf16[2,128,128]{2,1,0:T(8,128)(2,1)}, u32[]{:S(2)}) copy-start(bf16[2,128,128]{2,1,0:T(8,128)(2,1)} %param.15) | copy-start | bytes 196612
  116.3 28.0 %all-to-all-start.1 = ((bf16[16,8,4096]{2,1,0:T(8,128)(2,1)}), bf16[16,8,4096]{2,1,0:T(8,128)(2,1)S(1)}, u32[]{:S(2)}, u32[]{:S(2)}) async-start(bf16[16,8,4096]{2,1,0:T(8,128)(2,1)} %reshape.328), calls=%async_computation.1 | async-start | bytes 2097152 | tf_op jit(solution)/shard_map/all_to_all | solution.py:110
  148.1 373.2 %copy-start.30 = (f32[4096]{0:T(1024)}, f32[4096]{0:T(1024)S(1)}, u32[]{:S(2)}) copy-start(f32[4096]{0:T(1024)S(1)} %broadcast_multiply_fusion.10) | copy-start | bytes 49156
  149.4 371.9 %copy-start.32 = (f32[4096]{0:T(1024)}, f32[4096]{0:T(1024)S(1)}, u32[]{:S(2)}) copy-start(f32[4096]{0:T(1024)S(1)} %add_rsqrt_fusion.1) | copy-start | bytes 49156
  259.9 28.1 %all-to-all-start.3 = ((bf16[16,8,4096]{2,1,0:T(8,128)(2,1)}), bf16[16,8,4096]{2,1,0:T(8,128)(2,1)}, u32[]{:S(2)}, u32[]{:S(2)}) async-start(bf16[16,8,4096]{2,1,0:T(8,128)(2,1)} %reshape.333), calls=%async_computation.3 | async-start | bytes 2097152 | tf_op jit(solution)/shard_map/all_to_all | solution.py:110
  364.0 46.4 %all-to-all-start.5 = ((bf16[16,16,4096]{2,1,0:T(8,128)(2,1)}), bf16[16,16,4096]{2,1,0:T(8,128)(2,1)}, u32[]{:S(2)}, u32[]{:S(2)}) async-start(bf16[16,16,4096]{2,1,0:T(8,128)(2,1)} %reshape.338), calls=%async_computation.5 | async-start | bytes 4194304 | tf_op jit(solution)/shard_map/all_to_all | solution.py:110
  430.4 4.4 copy-start.7
  430.4 4.3 copy-start.44
  430.4 4.3 copy-start.46
  430.4 4.3 copy-start.56
  430.5 4.3 copy-start.63
  509.9 46.4 %all-to-all-start.7 = ((bf16[16,16,4096]{2,1,0:T(8,128)(2,1)}), bf16[16,16,4096]{2,1,0:T(8,128)(2,1)}, u32[]{:S(2)}, u32[]{:S(2)}) async-start(bf16[16,16,4096]{2,1,0:T(8,128)(2,1)} %reshape.344), calls=%async_computation.7 | async-start | bytes 4194304 | tf_op jit(solution)/shard_map/all_to_all | solution.py:110
  515.1 6.3 %copy-start.27 = (bf16[128,4096]{0,1:T(8,128)(2,1)S(1)}, bf16[128,4096]{0,1:T(8,128)(2,1)}, u32[]{:S(2)}) copy-start(bf16[128,4096]{0,1:T(8,128)(2,1)} %copy-done.26) | copy-start | bytes 3145732
  565.0 5.1 copy-start.10
  572.3 4.2 copy-start.39
  576.7 31.3 %copy-start.5 = (f32[4096,128]{1,0:T(8,128)S(1)}, f32[4096,128]{1,0:T(8,128)}, u32[]{:S(2)}) copy-start(f32[4096,128]{1,0:T(8,128)} %fusion.9) | copy-start | bytes 6291460
  576.7 31.3 %copy-start.60 = (f32[128]{0:T(128)S(1)}, f32[128]{0:T(128)}, u32[]{:S(2)}) copy-start(f32[128]{0:T(128)} %get-tuple-element.66) | copy-start | bytes 1540
  577.7 30.4 %copy-start.31 = (f32[4096]{0:T(1024)S(1)}, f32[4096]{0:T(1024)}, u32[]{:S(2)}) copy-start(f32[4096]{0:T(1024)} %copy-done.30) | copy-start | bytes 49156
  577.7 30.4 %copy-start.33 = (f32[4096]{0:T(1024)S(1)}, f32[4096]{0:T(1024)}, u32[]{:S(2)}) copy-start(f32[4096]{0:T(1024)} %copy-done.32) | copy-start | bytes 49156
  577.7 30.4 %copy-start.35 = (f32[4096]{0:T(1024)S(1)}, f32[4096]{0:T(1024)}, u32[]{:S(2)}) copy-start(f32[4096]{0:T(1024)} %copy-done.34) | copy-start | bytes 49156
  577.7 30.4 %copy-start.38 = (f32[4096]{0:T(1024)S(1)}, f32[4096]{0:T(1024)}, u32[]{:S(2)}) copy-start(f32[4096]{0:T(1024)} %copy-done.37) | copy-start | bytes 49156
  577.7 30.4 %copy-start.45 = (f32[4096]{0:T(1024)S(1)}, f32[4096]{0:T(1024)}, u32[]{:S(2)}) copy-start(f32[4096]{0:T(1024)} %copy-done.44) | copy-start | bytes 49156
  577.7 30.4 %copy-start.47 = (f32[4096]{0:T(1024)S(1)}, f32[4096]{0:T(1024)}, u32[]{:S(2)}) copy-start(f32[4096]{0:T(1024)} %copy-done.46) | copy-start | bytes 49156
  577.7 24.2 %all-to-all-start.8 = ((bf16[16,97,128]{2,1,0:T(8,128)(2,1)}), bf16[16,97,128]{2,1,0:T(8,128)(2,1)}, u32[]{:S(2)}, u32[]{:S(2)}) async-start(bf16[16,97,128]{2,1,0:T(8,128)(2,1)} %reshape.347), calls=%async_computation.8 | async-start | bytes 851968 | tf_op jit(solution)/shard_map/all_to_all | solution.py:110
  603.8 17.0 %all-to-all-start.9 = ((bf16[16,97,128]{2,1,0:T(8,128)(2,1)}), bf16[16,97,128]{2,1,0:T(8,128)(2,1)}, u32[]{:S(2)}, u32[]{:S(2)}) async-start(bf16[16,97,128]{2,1,0:T(8,128)(2,1)} %broadcast_in_dim.14), calls=%async_computation.9 | async-start | bytes 851968 | tf_op jit(solution)/shard_map/all_to_all | solution.py:110
  (48 other events, 132.7 us)
